TPU v7x, 256 devices: a whole 4x4x8 slice. The times are simulated.
256 devices in a mesh: fsdp: 4 (over y), tp: 64 (over z, x, core).
Axes of the slice: x: 4, y: 4, z: 8, core: 2. Of those that a mesh axis runs over, the one named last changes fastest.
Arguments:
- tokens: bfloat16 [512, 8192], P('tp', 'fsdp'), may hold values from -6 to 6
- gate_weight: bfloat16 [8192, 28672], P('fsdp', 'tp'), may hold values from -0.09375 to 0.09375
- up_weight: bfloat16 [8192, 28672], P('fsdp', 'tp'), may hold values from -0.09375 to 0.09375
- down_weight: bfloat16 [28672, 8192], P('tp', 'fsdp'), may hold values from -0.0625 to 0.0625
- gate_mask: int32 [128, 448], P('fsdp', 'tp'), may hold values 0 or 1
- up_mask: int32 [128, 448], P('fsdp', 'tp'), may hold values 0 or 1
- down_mask: int32 [448, 128], P('tp', 'fsdp'), may hold values 0 or 1
- grad_out: bfloat16 [512, 8192], P('tp', 'fsdp'), may hold values from -6 to 6
Outputs:
- output: bfloat16 [512, 8192], P('tp', 'fsdp')
- grad_tokens: bfloat16 [512, 8192], P('tp', 'fsdp')
- grad_gate: bfloat16 [8192, 28672], P('fsdp', 'tp')
- grad_up: bfloat16 [8192, 28672], P('fsdp', 'tp')
- grad_down: bfloat16 [28672, 8192], P('tp', 'fsdp')
All inputs are finite; a program needn't handle non-finite values. No bound on the sum of `gate_mask` or of `up_mask` or of `down_mask` on one device may be relied on, other than what follows from the above.
Results may differ from a plain program's by a relative error of at most 0.0049.
Values may be sent and summed in bfloat16 or wider, within the bound.
A program may use at most 128 MiB of HBM per device.

v0:
```python
import jax
import jax.numpy as jnp
from jax import lax
from jax.sharding import PartitionSpec as P

BLOCK = 64


def expand(mask, dtype):
    return jnp.repeat(jnp.repeat(mask, BLOCK, axis=0), BLOCK, axis=1).astype(dtype)


def contract_rows(left, right):
    return lax.dot_general(
        left, right, (((0,), (0,)), ((), ())), preferred_element_type=jnp.float32
    )


def contract_cols(left, right):
    return lax.dot_general(
        left, right, (((1,), (1,)), ((), ())), preferred_element_type=jnp.float32
    )


def activate(gate_value, up_value):
    sigmoid_gate = jax.nn.sigmoid(gate_value)
    activated = gate_value * sigmoid_gate
    return (activated * up_value).astype(jnp.bfloat16)


def backprop(grad_hidden, gate_value, up_value):
    sigmoid_gate = jax.nn.sigmoid(gate_value)
    activated = gate_value * sigmoid_gate
    grad_gate_value = (
        grad_hidden * up_value * sigmoid_gate * (1.0 + gate_value * (1.0 - sigmoid_gate))
    ).astype(jnp.bfloat16)
    grad_up_value = (grad_hidden * activated).astype(jnp.bfloat16)
    return (grad_gate_value, grad_up_value)


def body(tokens, gate_weight, up_weight, down_weight, gate_mask, up_mask, down_mask, grad_out):
    gate_full = expand(gate_mask, gate_weight.dtype)
    up_full = expand(up_mask, up_weight.dtype)
    down_full = expand(down_mask, down_weight.dtype)
    gate_kept = gate_weight * gate_full
    up_kept = up_weight * up_full
    down_kept = down_weight * down_full
    all_tokens = lax.all_gather(tokens, "tp", axis=0, tiled=True)
    gate_part = jnp.dot(all_tokens, gate_kept, preferred_element_type=jnp.float32)
    up_part = jnp.dot(all_tokens, up_kept, preferred_element_type=jnp.float32)
    gate_value, up_value = (
        lax.psum_scatter(gate_part, "fsdp", scatter_dimension=0, tiled=True),
        lax.psum_scatter(up_part, "fsdp", scatter_dimension=0, tiled=True),
    )
    hidden_slab = activate(gate_value, up_value)
    hidden = lax.all_gather(hidden_slab, "fsdp", axis=0, tiled=True)
    output = lax.psum_scatter(
        jnp.dot(hidden, down_kept, preferred_element_type=jnp.float32),
        "tp",
        scatter_dimension=0,
        tiled=True,
    ).astype(jnp.bfloat16)
    all_cotangent = lax.all_gather(grad_out, "tp", axis=0, tiled=True)
    hidden_part = contract_cols(all_cotangent, down_kept)
    grad_hidden = lax.psum_scatter(hidden_part, "fsdp", scatter_dimension=0, tiled=True)
    gate_slab, up_slab = backprop(grad_hidden, gate_value, up_value)
    grad_gate_value, grad_up_value = (
        lax.all_gather(gate_slab, "fsdp", axis=0, tiled=True),
        lax.all_gather(up_slab, "fsdp", axis=0, tiled=True),
    )
    grad_tokens = lax.psum_scatter(
        contract_cols(grad_gate_value, gate_kept) + contract_cols(grad_up_value, up_kept),
        "tp",
        scatter_dimension=0,
        tiled=True,
    ).astype(jnp.bfloat16)
    grad_down = (contract_rows(hidden, all_cotangent) * down_full).astype(jnp.bfloat16)
    grad_gate = (contract_rows(all_tokens, grad_gate_value) * gate_full).astype(jnp.bfloat16)
    grad_up = (contract_rows(all_tokens, grad_up_value) * up_full).astype(jnp.bfloat16)
    return (output, grad_tokens, grad_gate, grad_up, grad_down)


def solution(mesh):
    placed = (
        P("tp", "fsdp"),
        P("fsdp", "tp"),
        P("fsdp", "tp"),
        P("tp", "fsdp"),
        P("fsdp", "tp"),
        P("fsdp", "tp"),
        P("tp", "fsdp"),
        P("tp", "fsdp"),
    )
    return jax.shard_map(
        body,
        mesh=mesh,
        in_specs=placed,
        out_specs=(
            P("tp", "fsdp"),
            P("tp", "fsdp"),
            P("fsdp", "tp"),
            P("fsdp", "tp"),
            P("tp", "fsdp"),
        ),
        check_vma=False,
    )
```

profile of v0, /device:TPU:1, one launch (start us, length us, event | category | flops | bytes accessed | tf_op | source)
XLA Modules:
  0.0 604.9 jit_solution(5987199874716234783)
XLA Ops:
  7.2 0.7 all-gather.3.cloned.1.call-update
  7.9 0.7 all-gather.5.cloned.1.call-update
  8.7 0.7 convert_element_type.66
  9.6 1.6 bitcast_multiply_fusion.3
  11.3 80.9 %all-gather.3.cloned.1.call-done = bf16[512,2048]{1,0:T(8,128)(2,1)} async-done(((bf16[8,2048]{1,0:T(8,128)(2,1)}), bf16[512,2048]{1,0:T(8,128)(2,1)}) %all-gather.3.cloned.1.call-update) | async-done | bytes 2097168 | tf_op jit(solution)/shard_map/all_gather | solution.py:48
  92.2 3.7 convolution_bitcast_fusion.2
  96.3 1.6 bitcast_multiply_fusion.2
  97.9 1.2 copy-done
  99.1 3.8 convolution_bitcast_fusion.1
  103.4 2.5 copy.20
  105.9 1.7 bitcast_multiply_fusion.4
  107.6 62.4 %all-gather.5.cloned.1.call-done = bf16[512,2048]{1,0:T(8,128)(2,1)} async-done(((bf16[8,2048]{1,0:T(8,128)(2,1)}), bf16[512,2048]{1,0:T(8,128)(2,1)}) %all-gather.5.cloned.1.call-update) | async-done | bytes 2097168 | tf_op jit(solution)/shard_map/all_gather | solution.py:63
  170.0 4.0 convolution_bitcast_fusion
  174.0 1.5 broadcast_in_dim.23
  175.5 3.9 copy.21
  179.4 0.6 dynamic-slice
  180.6 13.3 %reduce-scatter.4.cloned.1.call-done = f32[128,448]{0,1:T(8,128)} async-done(((f32[512,448]{0,1:T(8,128)}), f32[128,448]{0,1:T(8,128)}) %reduce-scatter.4.cloned.1.call-update) | async-done | bytes 229392 | tf_op jit(solution)/shard_map/reduce_scatter | solution.py:52
  194.0 27.7 %reduce-scatter.6.cloned.1.call-done = f32[128,448]{0,1:T(8,128)} async-done(((f32[512,448]{0,1:T(8,128)}), f32[128,448]{0,1:T(8,128)}) %reduce-scatter.6.cloned.1.call-update) | async-done | bytes 229392 | tf_op jit(solution)/shard_map/reduce_scatter | solution.py:53
  221.7 28.3 %reduce-scatter.8.cloned.1.call-done = f32[128,448]{0,1:T(8,128)} async-done(((f32[512,448]{0,1:T(8,128)}), f32[128,448]{0,1:T(8,128)}) %reduce-scatter.8.cloned.1.call-update) | async-done | bytes 229392 | tf_op jit(solution)/shard_map/reduce_scatter | solution.py:65
  250.0 1.3 multiply_convert_fusion.1
  251.3 10.6 %all_gather.19 = bf16[512,448]{0,1:T(8,128)(2,1)S(1)} all-gather(bf16[128,448]{0,1:T(8,128)(2,1)S(1)} %get-tuple-element.7), channel_id=1, replica_groups=mesh['fsdp'=4,'tp'=64] {'fsdp'}, dimensions={0}, use_global_device_ids=true | all-gather | bytes 573440 | tf_op jit(solution)/shard_map/all_gather | solution.py:69
  261.9 10.6 %all_gather.18 = bf16[512,448]{0,1:T(8,128)(2,1)S(1)} all-gather(bf16[128,448]{0,1:T(8,128)(2,1)S(1)} %get-tuple-element.8), channel_id=1, replica_groups=mesh['fsdp'=4,'tp'=64] {'fsdp'}, dimensions={0}, use_global_device_ids=true | all-gather | bytes 573440 | tf_op jit(solution)/shard_map/all_gather | solution.py:68
  272.6 10.4 %all_gather.16 = bf16[512,448]{0,1:T(8,128)(2,1)S(1)} all-gather(bf16[128,448]{0,1:T(8,128)(2,1)S(1)} %get-tuple-element.9), channel_id=1, replica_groups=mesh['fsdp'=4,'tp'=64] {'fsdp'}, dimensions={0}, use_global_device_ids=true | all-gather | bytes 573440 | tf_op jit(solution)/shard_map/all_gather | solution.py:56
  283.0 3.3 fusion.3
  286.3 1.3 fusion.4
  287.5 0.2 copy-done.1
  287.8 3.3 convolution_add_fusion
  291.1 296.6 %all-reduce.4 = (bf16[512,2048]{1,0:T(8,128)(2,1)S(1)}, bf16[512,2048]{1,0:T(8,128)(2,1)}) all-reduce(f32[512,2048]{1,0:T(8,128)} %fusion.3, f32[512,2048]{1,0:T(8,128)} %convolution_add_fusion), channel_id=4, replica_groups=mesh['fsdp'=4,'tp'=64] {'tp'}, use_global_device_ids=true, to_apply=%region_2.0.clone | all-reduce | flops 2097152 | bytes 12582912
  587.7 1.4 dynamic-slice_convert_fusion
  589.3 4.1 fusion
  593.7 2.4 fusion.1
  596.0 2.4 multiply_convert_fusion
  (39 shorter events, 1.5 us)
Async XLA Ops:
  7.2 85.0 %all-gather.3.cloned.1.call-start = ((), (), s32[]{:S(2)}) async-start(), calls=%async_computation.3 | async-start | bytes 2129920 | tf_op jit(solution)/shard_map/all_gather | solution.py:48
  7.9 162.1 %all-gather.5.cloned.1.call-start = ((), (), s32[]{:S(2)}) async-start(), calls=%async_computation.6 | async-start | bytes 2129920 | tf_op jit(solution)/shard_map/all_gather | solution.py:63
  8.6 185.3 %reduce-scatter.4.cloned.1.call-start = ((), (), s32[]{:S(2)}) async-start(), calls=%async_computation.4 | async-start | bytes 1146880 | tf_op jit(solution)/shard_map/reduce_scatter | solution.py:52
  11.2 84.7 %copy-start.2 = (bf16[2048,448]{0,1:T(8,128)(2,1)}, bf16[2048,448]{0,1:T(8,128)(2,1)S(1)}, u32[]{:S(2)}) copy-start(bf16[2048,448]{0,1:T(8,128)(2,1)S(1)} %bitcast_multiply_fusion.3) | copy-start | bytes 5505028
  11.3 84.8 %copy-start.6 = (s32[32,7]{0,1:T(8,128)S(1)}, s32[32,7]{0,1:T(8,128)}, u32[]{:S(2)}) copy-start(s32[32,7]{0,1:T(8,128)} %param.13) | copy-start | bytes 2692
  96.0 125.7 %reduce-scatter.6.cloned.1.call-start = ((), (), s32[]{:S(2)}) async-start(), calls=%async_computation.5 | async-start | bytes 1146880 | tf_op jit(solution)/shard_map/reduce_scatter | solution.py:53
  97.9 1.2 copy-start
  99.1 3.9 copy-start.7
  99.1 4.3 copy-start.4
  103.0 147.0 %reduce-scatter.8.cloned.1.call-start = ((), (), s32[]{:S(2)}) async-start(), calls=%async_computation.7 | async-start | bytes 1146880 | tf_op jit(solution)/shard_map/reduce_scatter | solution.py:65
  175.5 3.9 copy-start.10
  283.0 3.3 copy-start.3
  286.3 1.5 copy-start.1
  589.3 4.4 copy-start.8
  593.6 2.4 copy-start.5
  593.7 2.4 copy-start.9
Sparse Core Ops, SparseCore 0:
  10.8 81.3 all-gather.2
  95.0 74.9 all-gather.4
  172.6 21.3 reduce-scatter.3
  196.4 25.2 reduce-scatter.5
  224.7 25.2 reduce-scatter.7
where the time goes:
time: 609 us; the launch traced here: 605 us
  blocking collectives  328 us (54%)
  waiting for transfers between devices  214 us (35%)
  matrix products  28.3 us (5%)
  between operations  14.6 us (2%)
  local copies, waits for them, and re-layouts  12.5 us (2%)
  other arithmetic  7.01 us (1%)
    unnamed x1, blocking collectives  297 us
    all_gather x1, waiting for transfers between devices, body(): all_tokens = lax.all_gather(tokens, 'tp', axis=0, tiled=True)  80.9 us
    all_gather x1, waiting for transfers between devices, body(): all_cotangent = lax.all_gather(grad_out, 'tp', axis=0, tiled=True)  62.4 us
    reduce_scatter x1, waiting for transfers between devices, body(): lax.psum_scatter(hidden_part, 'fsdp', scatter_dimension=0, tiled=True)  28.3 us
    reduce_scatter x1, waiting for transfers between devices, body(): lax.psum_scatter(up_part, 'fsdp', scatter_dimension=0, tiled=True)  27.7 us
    reduce_scatter x1, waiting for transfers between devices, body(): lax.psum_scatter(gate_part, 'fsdp', scatter_dimension=0, tiled=True)  13.3 us
  transfers between devices with their start and end apart: 5, of which 5 were waited for; matrix products, arithmetic and copies ran while one was open for 4% of the time, Pallas kernels for 0%

commit v1 on v0

v1 whole, which is shorter than its diff:
```python
import jax
import jax.numpy as jnp
from jax import lax
from jax.experimental import pallas as pl
from jax.experimental.pallas import tpu as pltpu
from jax.sharding import PartitionSpec as P

NY, NZ, NX = 4, 8, 4
BLOCK = 64
TOK = 512
DL = 2048
FL = 448
SLAB = FL // NY
QW = DL // 4
HW = DL // 2
F32 = jnp.float32
BF16 = jnp.bfloat16
MESH = pl.DeviceIdType.MESH
N_SEMS = 160


def nt(left, right):
    return lax.dot_general(left, right, (((1,), (1,)), ((), ())), preferred_element_type=F32)


def kernel(
    tok_ref, cot_ref, wg_hbm, wu_hbm, wd_hbm, mg_ref, mu_ref, md_ref,
    out_ref, gtok_ref, gg_hbm, gu_hbm, gd_hbm,
    w, mx, xk, exs, exr, pf, sb, rb, act, full, tr,
    own, psend, precv, xsend, xrecv, x2send, x2recv, ring_s, ring_r,
    r0, r1, zsend, zrecv, fin, finr, gout,
    send_sem, recv_sem, loc_sem,
):
    f = lax.axis_index("fsdp")
    t = lax.axis_index("tp")
    z = t // (2 * NX)
    x = (t // 2) % NX
    c = t % 2
    o = 1 - c

    def at(dy=0, dz=0, dx=0, flip=False):
        core = o if flip else c
        zz = lax.rem(z + dz + NZ, NZ)
        xx = lax.rem(x + dx + NX, NX)
        return (lax.rem(f + dy, NY), zz * (2 * NX) + xx * 2 + core)

    partner = at(flip=True)
    peers = [at(dy=d) for d in range(1, NY)]
    peers += [at(dz=d) for d in range(1, NZ)]
    peers += [at(dx=d) for d in range(1, NX)]
    peers += [partner]

    barrier = pltpu.get_barrier_semaphore()
    for peer in peers:
        pl.semaphore_signal(barrier, inc=1, device_id=peer, device_id_type=MESH)

    loads = [
        pltpu.make_async_copy(src, w.at[i], loc_sem.at[i])
        for i, src in enumerate((wg_hbm, wu_hbm, wd_hbm))
    ]
    for load in loads:
        load.start()

    for a, ref in enumerate((tok_ref, cot_ref)):
        exs[a] = ref[:, pl.ds(pl.multiple_of(o * HW, HW), HW)].astype(F32)
    pl.semaphore_wait(barrier, len(peers))

    sent = []

    def send(src, dst, peer):
        i = len(sent)
        copy = pltpu.make_async_remote_copy(
            src_ref=src, dst_ref=dst, send_sem=send_sem.at[i], recv_sem=recv_sem.at[i],
            device_id=peer, device_id_type=MESH,
        )
        copy.start()
        sent.append(copy)
        return copy

    def zr(d):
        return lax.rem(z + d + NZ, NZ)

    def xr(d):
        return lax.rem(x + d + NX, NX)

    exchange = [send(exs.at[a], exr.at[a], partner) for a in range(2)]
    k0, k1 = 2 * c, 2 * c + 1

    q0x, q1z = [], []
    for a, ref in enumerate((tok_ref, cot_ref)):
        exchange[a].wait_recv()
        mine = ref[:, pl.ds(pl.multiple_of(c * HW, HW), HW)].astype(F32)
        theirs = exr[a]
        first = jnp.where(c == 0, mine, theirs)
        second = jnp.where(c == 0, theirs, mine)
        rows = jnp.concatenate([first, second], axis=0).astype(BF16)
        xk[a, k0, z, x] = rows[:, :QW]
        xk[a, k1, z, x] = rows[:, QW:]
        here = xk.at[a, k0, z, x]
        q0x.append([send(here, here, at(dx=d)) for d in (1, 3, 2)])
    for a in range(2):
        here = xk.at[a, k1, z, x]
        q1z.append([send(here, here, at(dz=d)) for d in (1, 7, 2, 6, 3, 5, 4)])

    feature_block = lax.broadcasted_iota(jnp.int32, (DL // BLOCK, DL), 1) // BLOCK
    block = lax.broadcasted_iota(jnp.int32, (DL // BLOCK, DL), 0)
    spread = (feature_block == block).astype(F32).astype(BF16)
    for i, ref in enumerate((mg_ref, mu_ref, md_ref)):
        mx[i, 0 : FL // BLOCK] = jnp.dot(
            ref[...].astype(F32).astype(BF16), spread, preferred_element_type=F32
        )

    def prune(i):
        loads[i].wait()

        @pl.loop(0, FL // BLOCK)
        def _(b):
            rows = pl.ds(pl.multiple_of(b * BLOCK, BLOCK), BLOCK)
            w[i, rows, :] = (w[i, rows, :].astype(F32) * mx[i, pl.ds(b, 1), :]).astype(BF16)

    fwd = []

    def forward(ref):
        fwd.append(send(ref, ref, partner))

    up, down = [[], []], [[], []]
    for a in range(2):
        for copy in q0x[a]:
            copy.wait_recv()
        here = xk.at[a, k0, z]
        up[a].append(send(here, here, at(dz=1)))
        down[a].append(send(here, here, at(dz=-1)))
        forward(here)
    prune(0)
    q1x = []
    for a in range(2):
        for copy in q1z[a]:
            copy.wait_recv()
        here = xk.at[a, k1, :, x]
        q1x.append([send(here, here, at(dx=d)) for d in (1, 3, 2)])
        forward(here)
    for hop in (1, 2, 3):
        for a in range(2):
            up[a][hop - 1].wait_recv()
            got = xk.at[a, k0, zr(-hop)]
            part = got if hop < 3 else xk.at[a, k0, zr(-hop), 0:2]
            up[a].append(send(part, part, at(dz=1)))
            forward(got)
            down[a][hop - 1].wait_recv()
            got = xk.at[a, k0, zr(hop)]
            part = got if hop < 3 else xk.at[a, k0, zr(hop), 2:4]
            down[a].append(send(part, part, at(dz=-1)))
            forward(got)
        if hop < 3:
            prune(hop)
    for a in range(2):
        for copy, d in zip(q1x[a], (1, 3, 2)):
            copy.wait_recv()
            forward(xk.at[a, k1, :, xr(-d)])
    for a in range(2):
        up[a][3].wait_recv()
        forward(xk.at[a, k0, zr(4), 0:2])
        down[a][3].wait_recv()
        forward(xk.at[a, k0, zr(4), 2:4])
    for copy in fwd:
        copy.wait_recv()

    def project(m, a):
        @pl.loop(0, 4)
        def _(i):
            rows = pl.ds(pl.multiple_of((i // 2) * (FL // 2), FL // 2), FL // 2)
            cols = pl.ds(pl.multiple_of((i % 2) * 256, 256), 256)
            zs = pl.ds((i % 2) * 4, 4)
            total = None
            for k in range(4):
                term = nt(
                    w[m, rows, k * QW : (k + 1) * QW],
                    xk[a, k, zs].reshape(256, QW),
                )
                total = term if total is None else total + term
            pf[m, rows, cols] = total
            sb[m, rows, cols] = total.astype(BF16)

    def scatter(m):
        copies = []
        for d in (1, 3, 2):
            theirs = pl.ds(pl.multiple_of(lax.rem(f + d, NY) * SLAB, 16), SLAB)
            copies.append(send(sb.at[m, theirs, :], rb.at[m, d - 1], at(dy=d)))
        return copies

    my_slab = pl.multiple_of(f * SLAB, 16)
    sums = []
    for m, a in ((0, 0), (1, 0), (2, 1)):
        project(m, a)
        sums.append(scatter(m))

    def summed(m, b):
        rows = pl.ds(pl.multiple_of(b * 16, 16), 16)
        total = pf[m, pl.ds(pl.multiple_of(my_slab + b * 16, 16), 16), :]
        for d in range(3):
            total = total + rb[m, d, rows, :].astype(F32)
        return total

    def gather(i):
        here = full.at[i, pl.ds(my_slab, SLAB), :]
        return [send(here, here, at(dy=d)) for d in (1, 3, 2)]

    for m in range(2):
        for copy in sums[m]:
            copy.wait_recv()

    @pl.loop(0, SLAB // 16)
    def _(b):
        rows = pl.ds(pl.multiple_of(b * 16, 16), 16)
        gate = summed(0, b)
        upv = summed(1, b)
        sig = 1.0 / (1.0 + jnp.exp(-gate))
        activated = gate * sig
        full[0, pl.ds(pl.multiple_of(my_slab + b * 16, 16), 16), :] = (activated * upv).astype(BF16)
        act[0, rows, :] = activated
        act[1, rows, :] = upv * sig * (1.0 + gate * (1.0 - sig))

    hidden = gather(0)
    for copy in sums[2]:
        copy.wait_recv()

    @pl.loop(0, SLAB // 16)
    def _(b):
        rows = pl.ds(pl.multiple_of(b * 16, 16), 16)
        mine = pl.ds(pl.multiple_of(my_slab + b * 16, 16), 16)
        grad_hidden = summed(2, b)
        full[1, mine, :] = (grad_hidden * act[1, rows, :]).astype(BF16)
        full[2, mine, :] = (grad_hidden * act[0, rows, :]).astype(BF16)

    grads = [gather(1), gather(2)]

    def turn(i):
        @pl.loop(0, TOK // 128)
        def _(b):
            cols = pl.ds(pl.multiple_of(b * 128, 128), 128)
            tr[i, cols, :] = full[i, :, cols].astype(F32).T.astype(BF16)

    def product(a, pairs):
        copies = []
        for half, dst in ((o, psend), (c, own)):
            for j in range(2):

                @pl.loop(0, HW // 256)
                def _(n):
                    cols = pl.ds(pl.multiple_of(half * HW + n * 256, 256), 256)
                    total = None
                    for i, m in pairs:
                        term = jnp.dot(
                            tr[i, j * 256 : (j + 1) * 256, :], w[m, :, cols],
                            preferred_element_type=F32,
                        )
                        total = term if total is None else total + term
                    dst[a, j * 4 : (j + 1) * 4, :, :, pl.ds(pl.multiple_of(n * 256, 256), 256)] = (
                        total.reshape(4, NX, 16, 256)
                    )

                if dst is psend:
                    part = pl.ds(j * 4, 4)
                    copies.append(send(psend.at[a, part], precv.at[a, part], partner))
        return copies

    stores = []

    def weight_grad(i, a, m, hbm):
        @pl.loop(0, 4)
        def _(k):
            cols = pl.ds(pl.multiple_of(k * QW, QW), QW)
            total = jnp.dot(full[i], xk[a, k].reshape(TOK, QW), preferred_element_type=F32)
            for b in range(FL // BLOCK):
                rows = slice(b * BLOCK, (b + 1) * BLOCK)
                gout[m, rows, cols] = (total[rows] * mx[m, b : b + 1, cols]).astype(BF16)

        store = pltpu.make_async_copy(gout.at[m], hbm, loc_sem.at[3 + m])
        store.start()
        stores.append(store)

    for copy in hidden:
        copy.wait_recv()
    turn(0)
    swap = [product(0, ((0, 2),))]
    weight_grad(0, 1, 2, gd_hbm)
    for i in range(2):
        for copy in grads[i]:
            copy.wait_recv()
        turn(1 + i)
    swap.append(product(1, ((1, 0), (2, 1))))

    def part(a, zz, xs, q):
        cols = slice(q * QW, (q + 1) * QW)
        return own[a, zz, xs, :, cols] + precv[a, zz, xs, :, cols]

    up, down, bulk = [[], []], [[], []], []
    for a in range(2):
        for copy in swap[a]:
            copy.wait_recv()
        ring_s[a, 0, 0, 0:2] = part(a, zr(4), slice(0, 2), 0).astype(BF16)
        up[a].append(send(ring_s.at[a, 0, 0, 0:2], ring_r.at[a, 0, 0, 0:2], at(dz=1)))
        ring_s[a, 1, 0, 0:2] = part(a, zr(4), slice(2, 4), 0).astype(BF16)
        down[a].append(send(ring_s.at[a, 1, 0, 0:2], ring_r.at[a, 1, 0, 0:2], at(dz=-1)))
    for a in range(2):
        copies = []
        for d in (2, 1, 3):
            xsend[a, d - 1] = part(a, slice(0, NZ), xr(d), 1).astype(BF16)
            copies.append(send(xsend.at[a, d - 1], xrecv.at[a, d - 1], at(dx=d)))
        bulk.append(copies)

    def hop_on(a, hop):
        for side, chain, sign in ((0, up, 1), (1, down, -1)):
            chain[a][hop - 1].wait_recv()
            to = zr(sign * (4 - hop))
            if hop == 1:
                lo, hi = (slice(0, 2), slice(2, 4)) if side == 0 else (slice(2, 4), slice(0, 2))
                ring_s[a, side, hop, lo] = (
                    part(a, to, lo, 0) + ring_r[a, side, 0, 0:2].astype(F32)
                ).astype(BF16)
                ring_s[a, side, hop, hi] = part(a, to, hi, 0).astype(BF16)
            else:
                ring_s[a, side, hop] = (
                    part(a, to, slice(0, 4), 0) + ring_r[a, side, hop - 1].astype(F32)
                ).astype(BF16)
            chain[a].append(
                send(ring_s.at[a, side, hop], ring_r.at[a, side, hop], at(dz=sign))
            )

    for a in range(2):
        hop_on(a, 1)
    weight_grad(1, 0, 0, gg_hbm)
    for a in range(2):
        hop_on(a, 2)
    weight_grad(2, 0, 1, gu_hbm)
    for a in range(2):
        hop_on(a, 3)

    small = []
    for a in range(2):
        for copy in bulk[a]:
            copy.wait_recv()
        total = part(a, slice(0, NZ), x, 1)
        for d in range(3):
            total = total + xrecv[a, d].astype(F32)
        r1[a] = total
        copies = []
        for d in (4, 3, 5, 2, 6, 1, 7):
            zsend[a, d - 1] = r1[a, zr(d)].astype(BF16)
            copies.append(send(zsend.at[a, d - 1], zrecv.at[a, d - 1], at(dz=d)))
        small.append(copies)

    last = []
    for a in range(2):
        up[a][3].wait_recv()
        down[a][3].wait_recv()
        r0[a] = part(a, z, slice(0, 4), 0) + ring_r[a, 0, 3].astype(F32) + ring_r[a, 1, 3].astype(F32)
        copies = []
        for d in (2, 1, 3):
            x2send[a, d - 1] = r0[a, xr(d)].astype(BF16)
            copies.append(send(x2send.at[a, d - 1], x2recv.at[a, d - 1], at(dx=d)))
        last.append(copies)

    final = []
    for a in range(2):
        for copy in last[a]:
            copy.wait_recv()
        total0 = r0[a, x]
        for d in range(3):
            total0 = total0 + x2recv[a, d].astype(F32)
        for copy in small[a]:
            copy.wait_recv()
        total1 = r1[a, z]
        for d in range(7):
            total1 = total1 + zrecv[a, d].astype(F32)
        fin[a, :, :, :QW] = total0.reshape(2, 8, QW)
        fin[a, :, :, QW:] = total1.reshape(2, 8, QW)
        final.append(send(fin.at[a, o], finr.at[a], partner))
    for a, ref in enumerate((out_ref, gtok_ref)):
        final[a].wait_recv()
        ref[:, pl.ds(pl.multiple_of(c * HW, HW), HW)] = fin[a, c].astype(BF16)
        ref[:, pl.ds(pl.multiple_of(o * HW, HW), HW)] = finr[a].astype(BF16)

    for copy in sent:
        copy.wait_send()
    for store in stores:
        store.wait()


def body(tokens, gate_weight, up_weight, down_weight, gate_mask, up_mask, down_mask, grad_out):
    vmem = pl.BlockSpec(memory_space=pltpu.VMEM)
    hbm = pl.BlockSpec(memory_space=pl.ANY)
    out, gtok, gg, gu, gd = pl.pallas_call(
        kernel,
        name="ffn",
        out_shape=(
            jax.ShapeDtypeStruct((8, DL), BF16),
            jax.ShapeDtypeStruct((8, DL), BF16),
            jax.ShapeDtypeStruct((FL, DL), BF16),
            jax.ShapeDtypeStruct((FL, DL), BF16),
            jax.ShapeDtypeStruct((FL, DL), BF16),
        ),
        in_specs=[vmem, vmem, hbm, hbm, hbm, vmem, vmem, vmem],
        out_specs=(vmem, vmem, hbm, hbm, hbm),
        scratch_shapes=[
            pltpu.VMEM((3, FL, DL), BF16),
            pltpu.VMEM((3, 8, DL), F32),
            pltpu.VMEM((2, 4, NZ, NX, 16, QW), BF16),
            pltpu.VMEM((2, 8, HW), F32),
            pltpu.VMEM((2, 8, HW), F32),
            pltpu.VMEM((3, FL, TOK), F32),
            pltpu.VMEM((3, FL, TOK), BF16),
            pltpu.VMEM((3, 3, SLAB, TOK), BF16),
            pltpu.VMEM((2, SLAB, TOK), F32),
            pltpu.VMEM((3, FL, TOK), BF16),
            pltpu.VMEM((3, TOK, FL), BF16),
            pltpu.VMEM((2, NZ, NX, 16, HW), F32),
            pltpu.VMEM((2, NZ, NX, 16, HW), F32),
            pltpu.VMEM((2, NZ, NX, 16, HW), F32),
            pltpu.VMEM((2, 3, NZ, 16, QW), BF16),
            pltpu.VMEM((2, 3, NZ, 16, QW), BF16),
            pltpu.VMEM((2, 3, 16, QW), BF16),
            pltpu.VMEM((2, 3, 16, QW), BF16),
            pltpu.VMEM((2, 2, 4, NX, 16, QW), BF16),
            pltpu.VMEM((2, 2, 4, NX, 16, QW), BF16),
            pltpu.VMEM((2, NX, 16, QW), F32),
            pltpu.VMEM((2, NZ, 16, QW), F32),
            pltpu.VMEM((2, 7, 16, QW), BF16),
            pltpu.VMEM((2, 7, 16, QW), BF16),
            pltpu.VMEM((2, 2, 8, HW), F32),
            pltpu.VMEM((2, 8, HW), F32),
            pltpu.VMEM((3, FL, DL), BF16),
            pltpu.SemaphoreType.DMA((N_SEMS,)),
            pltpu.SemaphoreType.DMA((N_SEMS,)),
            pltpu.SemaphoreType.DMA((6,)),
        ],
        compiler_params=pltpu.CompilerParams(
            collective_id=0, has_side_effects=True, vmem_limit_bytes=56 * 2**20
        ),
    )(
        tokens, grad_out, gate_weight.T, up_weight.T, down_weight,
        gate_mask.T, up_mask.T, down_mask,
    )
    return out, gtok, gg.T, gu.T, gd


def solution(mesh):
    placed = (
        P("tp", "fsdp"),
        P("fsdp", "tp"),
        P("fsdp", "tp"),
        P("tp", "fsdp"),
        P("fsdp", "tp"),
        P("fsdp", "tp"),
        P("tp", "fsdp"),
        P("tp", "fsdp"),
    )
    return jax.shard_map(
        body,
        mesh=mesh,
        in_specs=placed,
        out_specs=(
            P("tp", "fsdp"),
            P("tp", "fsdp"),
            P("fsdp", "tp"),
            P("fsdp", "tp"),
            P("tp", "fsdp"),
        ),
        check_vma=False,
    )
```

time: 609 us -> 110 us (0.18)
  blocking collectives: 328 us -> 0 us
  waiting for transfers between devices: 214 us -> 0 us
  Pallas kernels: 0 us -> 100 us
  matrix products: 28.3 us -> 0 us
  between operations: 14.6 us -> 0.65 us
  other arithmetic: 7.01 us -> 0 us
    unnamed x1 -> x0, blocking collectives: 297 us -> none
    all_gather x2 -> x0, waiting for transfers between devices: 143 us -> none  [the longest x1 80.9 us: body(): all_tokens = lax.all_gather(tokens, 'tp', axis=0, tiled=True)]
    pallas_call x0 -> x1, Pallas kernels: none -> 100 us  [body(): pl.pallas_call(kernel, name='ffn', out_shape=(jax.ShapeDtypeStruct((8, DL...]
    reduce_scatter x3 -> x0, waiting for transfers between devices: 69.4 us -> none  [the longest x1 28.3 us: body(): lax.psum_scatter(hidden_part, 'fsdp', scatter_dimension=0, tiled=True)]
    all_gather x3 -> x0, blocking collectives: 31.6 us -> none  [the longest x1 10.6 us: body(): lax.all_gather(up_slab, 'fsdp', axis=0, tiled=True)]
    dot_general x9 -> x0, matrix products: 28.3 us -> none  [the longest x3 8.85 us: contract_rows(): lax.dot_general(left, right, (((0,), (0,)), ((), ())), preferred_element_...]
  transfers between devices with their start and end apart: 5 -> 0, of which waited for: 5 -> 0; matrix products, arithmetic and copies ran while one was open for 4% -> 0% of each run, Pallas kernels for 0% -> 0%
where the time goes in v1:
time: 110 us
  Pallas kernels  100 us (91%)
  local copies, waits for them, and re-layouts  9.21 us (8%)
    pallas_call x1, Pallas kernels, body(): pl.pallas_call(kernel, name='ffn', out_shape=(jax.ShapeDtypeStruct((8, DL...  100 us
    unnamed x9, local copies, waits for them, and re-layouts  9.21 us

profile of v1, /device:TPU:1, one launch (start us, length us, event | category | flops | bytes accessed | tf_op | source)
XLA Modules:
  0.0 109.8 jit_solution(6777510565082026393)
XLA Ops:
  0.6 100.0 %ffn.1 = (bf16[8,2048]{1,0:T(8,128)(2,1)}, bf16[8,2048]{1,0:T(8,128)(2,1)}, bf16[448,2048]{1,0:T(8,128)(2,1)}, bf16[448,2048]{1,0:T(8,128)(2,1)}, bf16[448,2048]{1,0:T(8,128)(2,1)}) custom-call(bf16[8,2048]{1,0:T(8,128)(2,1)} %tok_ref.1, bf16[8,2048]{1,0:T(8,128)(2,1)} %cot_ref.1, bf16[448,2048]{1,0:T(8,128)(2,1)} %bitcast.8, bf16[448,2048]{1,0:T(8,128)(2,1)} %bitcast.9, ...), custom_call_target="tpu_custom_call" | custom-call | tf_op jit(solution)/shard_map/ffn/pallas_call | solution.py:393
  100.6 1.4 %copy.18 = bf16[8,2048]{1,0:T(8,128)(2,1)} copy(bf16[8,2048]{1,0:T(8,128)(2,1)} %get-tuple-element.20) | data formatting | bytes 65536
  102.0 1.4 %copy.19 = bf16[8,2048]{1,0:T(8,128)(2,1)} copy(bf16[8,2048]{1,0:T(8,128)(2,1)} %get-tuple-element.21) | data formatting | bytes 65536
  103.4 0.0 copy-start.1
  103.4 3.1 %copy.20 = bf16[2048,448]{0,1:T(8,128)(2,1)} copy(bf16[2048,448]{0,1:T(8,128)(2,1)} %bitcast.7) | data formatting | bytes 3670016
  106.4 0.0 copy-done.1
  106.4 0.0 copy-start
  106.4 1.2 %copy.21 = bf16[2048,448]{0,1:T(8,128)(2,1)} copy(bf16[2048,448]{0,1:T(8,128)(2,1)S(1)} %bitcast.6) | data formatting | bytes 3670016
  107.7 0.9 copy-done
  108.6 1.2 %copy.22 = bf16[448,2048]{1,0:T(8,128)(2,1)} copy(bf16[448,2048]{1,0:T(8,128)(2,1)S(1)} %copy-done) | data formatting | bytes 3670016
Async XLA Ops:
  103.4 3.1 %copy-start.1 = (bf16[448,2048]{1,0:T(8,128)(2,1)S(1)}, bf16[448,2048]{1,0:T(8,128)(2,1)}, u32[]{:S(2)}) copy-start(bf16[448,2048]{1,0:T(8,128)(2,1)} %get-tuple-element.13) | copy-start | bytes 5505028
  106.4 2.2 %copy-start = (bf16[448,2048]{1,0:T(8,128)(2,1)S(1)}, bf16[448,2048]{1,0:T(8,128)(2,1)}, u32[]{:S(2)}) copy-start(bf16[448,2048]{1,0:T(8,128)(2,1)} %get-tuple-element.24) | copy-start | bytes 5505028

commit v2 on v1

v2 whole, which is shorter than its diff:
```python
import jax
import jax.numpy as jnp
from jax import lax
from jax.experimental import pallas as pl
from jax.experimental.pallas import tpu as pltpu
from jax.sharding import PartitionSpec as P

NY, NZ, NX = 4, 8, 4
BLOCK = 64
TOK = 512
DL = 2048
FL = 448
SLAB = FL // NY
QW = DL // 4
HW = DL // 2
F32 = jnp.float32
BF16 = jnp.bfloat16
MESH = pl.DeviceIdType.MESH
N_SEMS = 160
VMEM = 57 * 2**20


def nt(left, right):
    return lax.dot_general(left, right, (((1,), (1,)), ((), ())), preferred_element_type=F32)


def kernel(
    tok_hbm, cot_hbm, wg_hbm, wu_hbm, wd_hbm, mg_hbm, mu_hbm, md_hbm,
    out_ref, gtok_ref, gg_hbm, gu_hbm, gd_hbm,
    rows_in, masks_in, w, mx, xk, exs, exr, pf, sb, rb, act, full, tr,
    own, psend, precv, xsend, xrecv, x2send, x2recv, ring_s, ring_r,
    r0, r1, zsend, zrecv, fin, finr, gout,
    send_sem, recv_sem, loc_sem,
):
    f = lax.axis_index("fsdp")
    t = lax.axis_index("tp")
    z = t // (2 * NX)
    x = (t // 2) % NX
    c = t % 2
    o = 1 - c

    def at(dy=0, dz=0, dx=0, flip=False):
        core = o if flip else c
        zz = lax.rem(z + dz + NZ, NZ)
        xx = lax.rem(x + dx + NX, NX)
        return (lax.rem(f + dy + NY, NY), zz * (2 * NX) + xx * 2 + core)

    partner = at(flip=True)
    peers = [at(dy=d) for d in range(1, NY)]
    peers += [at(dz=d) for d in range(1, NZ)]
    peers += [at(dx=d) for d in range(1, NX)]
    peers += [partner]

    barrier = pltpu.get_barrier_semaphore()
    for peer in peers:
        pl.semaphore_signal(barrier, inc=1, device_id=peer, device_id_type=MESH)

    tokens_in = [
        pltpu.make_async_copy(src, rows_in.at[a], loc_sem.at[6 + a])
        for a, src in enumerate((tok_hbm, cot_hbm))
    ]
    blocks_in = [
        pltpu.make_async_copy(src, masks_in.at[i], loc_sem.at[8 + i])
        for i, src in enumerate((mg_hbm, mu_hbm, md_hbm))
    ]
    loads = [
        pltpu.make_async_copy(src, w.at[i], loc_sem.at[i])
        for i, src in enumerate((wg_hbm, wu_hbm, wd_hbm))
    ]
    loads = tokens_in + blocks_in + loads
    for load in loads:
        load.start()

    for a in range(2):
        loads[a].wait()
        exs[a] = rows_in[a, :, pl.ds(pl.multiple_of(o * HW, HW), HW)].astype(F32)
    pl.semaphore_wait(barrier, len(peers))

    sent = []

    def send(src, dst, peer):
        i = len(sent)
        copy = pltpu.make_async_remote_copy(
            src_ref=src, dst_ref=dst, send_sem=send_sem.at[i], recv_sem=recv_sem.at[i],
            device_id=peer, device_id_type=MESH,
        )
        copy.start()
        sent.append(copy)
        return copy

    def zr(d):
        return lax.rem(z + d + NZ, NZ)

    def xr(d):
        return lax.rem(x + d + NX, NX)

    exchange = [send(exs.at[a], exr.at[a], partner) for a in range(2)]
    k0, k1 = 2 * c, 2 * c + 1

    q0x, q1z, q1x = [], [], [None, None]
    passed = [[[], []], [[], []]]

    def forward(a, q, ref):
        passed[a][q].append(send(ref, ref, partner))

    def build(a):
        exchange[a].wait_recv()
        mine = rows_in[a, :, pl.ds(pl.multiple_of(c * HW, HW), HW)].astype(F32)
        theirs = exr[a]
        first = jnp.where(c == 0, mine, theirs)
        second = jnp.where(c == 0, theirs, mine)
        rows = jnp.concatenate([first, second], axis=0).astype(BF16)
        xk[a, k0, z, x] = rows[:, :QW]
        xk[a, k1, z, x] = rows[:, QW:]
        here = xk.at[a, k0, z, x]
        q0x.append([send(here, here, at(dx=d)) for d in (1, 3, 2)])

    def over_z(a):
        here = xk.at[a, k1, z, x]
        q1z.append([send(here, here, at(dz=d)) for d in (1, 7, 2, 6, 3, 5, 4)])

    def over_x(a):
        for copy in q1z[a]:
            copy.wait_recv()
        here = xk.at[a, k1, :, x]
        q1x[a] = [send(here, here, at(dx=d)) for d in (1, 3, 2)]
        forward(a, 1, here)

    def over_x_done(a):
        for copy, d in zip(q1x[a], (1, 3, 2)):
            copy.wait_recv()
            forward(a, 1, xk.at[a, k1, :, xr(-d)])

    ring = [[[], []], [[], []]]

    def ring_start(a):
        for copy in q0x[a]:
            copy.wait_recv()
        here = xk.at[a, k0, z]
        ring[a][0].append(send(here, here, at(dz=1)))
        ring[a][1].append(send(here, here, at(dz=-1)))
        forward(a, 0, here)

    def ring_hop(a, hop):
        for side, sign in ((0, 1), (1, -1)):
            ring[a][side][hop - 1].wait_recv()
            got = xk.at[a, k0, zr(-sign * hop)]
            part = got
            if hop == 3:
                part = xk.at[a, k0, zr(-sign * hop), 2 * side : 2 * side + 2]
            ring[a][side].append(send(part, part, at(dz=sign)))
            forward(a, 0, got)

    def ring_done(a):
        for side in range(2):
            ring[a][side][3].wait_recv()
            forward(a, 0, xk.at[a, k0, zr(4), 2 * side : 2 * side + 2])

    def passed_on(a, q):
        for copy in passed[a][q]:
            copy.wait_recv()

    def spread_masks():
        feature_block = lax.broadcasted_iota(jnp.int32, (DL // BLOCK, DL), 1) // BLOCK
        block = lax.broadcasted_iota(jnp.int32, (DL // BLOCK, DL), 0)
        spread = (feature_block == block).astype(F32).astype(BF16)
        for i in range(3):
            loads[2 + i].wait()
            mx[i, 0 : FL // BLOCK] = jnp.dot(
                masks_in[i].astype(F32).astype(BF16), spread, preferred_element_type=F32
            )

    def prune(i):
        loads[5 + i].wait()

        @pl.loop(0, FL // BLOCK)
        def _(b):
            rows = pl.ds(pl.multiple_of(b * BLOCK, BLOCK), BLOCK)
            w[i, rows, :] = (w[i, rows, :].astype(F32) * mx[i, pl.ds(b, 1), :]).astype(BF16)

    def project(m, a, ks, last):
        @pl.loop(0, 4, unroll=True)
        def _(i):
            rows = pl.ds(pl.multiple_of((i // 2) * (FL // 2), FL // 2), FL // 2)
            cols = pl.ds(pl.multiple_of((i % 2) * 256, 256), 256)
            zs = pl.ds((i % 2) * 4, 4)
            total = pf[m, rows, cols] if len(ks) == 2 and last else None
            for k in ks:
                term = nt(
                    w[m, rows, k * QW : (k + 1) * QW],
                    xk[a, k, zs].reshape(256, QW),
                )
                total = term if total is None else total + term
            pf[m, rows, cols] = total
            if last:
                sb[m, rows, cols] = total.astype(BF16)

    def scatter(m):
        copies = []
        for d in (1, 3, 2):
            theirs = pl.ds(pl.multiple_of(lax.rem(f + d, NY) * SLAB, 16), SLAB)
            copies.append(send(sb.at[m, theirs, :], rb.at[m, d - 1], at(dy=d)))
        return copies

    build(0)
    spread_masks()
    ring_start(0)
    over_z(0)
    build(1)
    prune(0)
    ring_hop(0, 1)
    over_x(0)
    prune(1)
    ring_hop(0, 2)
    ring_start(1)
    ring_hop(0, 3)
    over_z(1)
    over_x_done(0)
    ring_hop(1, 1)
    passed_on(0, 1)
    project(0, 0, (1, 3), False)
    ring_done(0)
    passed_on(0, 0)
    project(0, 0, (0, 2), True)
    sums = [scatter(0)]
    over_x(1)
    ring_hop(1, 2)
    project(1, 0, (0, 1, 2, 3), True)
    sums.append(scatter(1))
    ring_hop(1, 3)
    prune(2)
    over_x_done(1)
    ring_done(1)
    passed_on(1, 0)
    passed_on(1, 1)
    project(2, 1, (0, 1, 2, 3), True)
    sums.append(scatter(2))

    my_slab = pl.multiple_of(f * SLAB, 16)
    def summed(m, b):
        rows = pl.ds(pl.multiple_of(b * 16, 16), 16)
        total = pf[m, pl.ds(pl.multiple_of(my_slab + b * 16, 16), 16), :]
        for d in range(3):
            total = total + rb[m, d, rows, :].astype(F32)
        return total

    def gather(i):
        here = full.at[i, pl.ds(my_slab, SLAB), :]
        return [send(here, here, at(dy=d)) for d in (1, -1)]

    def relay(i, near):
        copies = []
        for side, sign in ((0, 1), (1, -1)):
            near[side].wait_recv()
            rows = pl.ds(pl.multiple_of(lax.rem(f - sign + NY, NY) * SLAB, 16), SLAB)
            part = full.at[i, rows, pl.ds(side * (TOK // 2), TOK // 2)]
            copies.append(send(part, part, at(dy=sign)))
        return copies

    for m in range(2):
        for copy in sums[m]:
            copy.wait_recv()

    @pl.loop(0, SLAB // 16)
    def _(b):
        rows = pl.ds(pl.multiple_of(b * 16, 16), 16)
        gate = summed(0, b)
        upv = summed(1, b)
        sig = 1.0 / (1.0 + jnp.exp(-gate))
        activated = gate * sig
        full[0, pl.ds(pl.multiple_of(my_slab + b * 16, 16), 16), :] = (activated * upv).astype(BF16)
        act[0, rows, :] = activated
        act[1, rows, :] = upv * sig * (1.0 + gate * (1.0 - sig))

    near = [gather(0)]
    for copy in sums[2]:
        copy.wait_recv()

    @pl.loop(0, SLAB // 16)
    def _(b):
        rows = pl.ds(pl.multiple_of(b * 16, 16), 16)
        mine = pl.ds(pl.multiple_of(my_slab + b * 16, 16), 16)
        grad_hidden = summed(2, b)
        full[1, mine, :] = (grad_hidden * act[1, rows, :]).astype(BF16)
        full[2, mine, :] = (grad_hidden * act[0, rows, :]).astype(BF16)

    near.append(gather(1))
    far = [relay(0, near[0])]
    near.append(gather(2))
    far.append(relay(1, near[1]))

    def turn(i):
        @pl.loop(0, TOK // 128)
        def _(b):
            cols = pl.ds(pl.multiple_of(b * 128, 128), 128)
            tr[i, cols, :] = full[i, :, cols].astype(F32).T.astype(BF16)

    def product(a, pairs):
        copies = []
        for half, dst in ((o, psend), (c, own)):
            for step in range(2):
                j = lax.rem(z // 4 + 1 + step, 2)
                rows = pl.ds(pl.multiple_of(j * 256, 256), 256)
                zs = pl.ds(j * 4, 4)

                @pl.loop(0, HW // 256, unroll=True)
                def _(n):
                    cols = pl.ds(pl.multiple_of(half * HW + n * 256, 256), 256)
                    total = None
                    for i, m in pairs:
                        term = jnp.dot(
                            tr[i, rows, :], w[m, :, cols],
                            preferred_element_type=F32,
                        )
                        total = term if total is None else total + term
                    dst[a, zs, :, :, pl.ds(pl.multiple_of(n * 256, 256), 256)] = (
                        total.reshape(4, NX, 16, 256)
                    )

                if dst is psend:
                    copies.append(send(psend.at[a, zs], precv.at[a, zs], partner))
        return copies

    stores = []

    def weight_grad(i, a, m, dst, half):
        @pl.loop(2 * half, 2 * half + 2, unroll=True)
        def _(k):
            cols = pl.ds(pl.multiple_of(k * QW, QW), QW)
            total = jnp.dot(full[i], xk[a, k].reshape(TOK, QW), preferred_element_type=F32)
            for b in range(FL // BLOCK):
                rows = slice(b * BLOCK, (b + 1) * BLOCK)
                gout[m, rows, cols] = (total[rows] * mx[m, b : b + 1, cols]).astype(BF16)

        if half == 1:
            store = pltpu.make_async_copy(gout.at[m], dst, loc_sem.at[3 + m])
            store.start()
            stores.append(store)

    def part(a, zz, xs, q):
        cols = slice(q * QW, (q + 1) * QW)
        return own[a, zz, xs, :, cols] + precv[a, zz, xs, :, cols]

    swap, bulk, small, last, final = ([None, None] for _ in range(5))
    chain = [[[], []], [[], []]]

    def reduce_start(a):
        swap[a][0].wait_recv()
        for side, sign in ((0, 1), (1, -1)):
            ring_s[a, side, 0, 0:2] = part(a, zr(4), slice(2 * side, 2 * side + 2), 0).astype(BF16)
            chain[a][side].append(
                send(ring_s.at[a, side, 0, 0:2], ring_r.at[a, side, 0, 0:2], at(dz=sign))
            )
        swap[a][1].wait_recv()
        bulk[a] = []
        for d in (2, 1, 3):
            xsend[a, d - 1] = part(a, slice(0, NZ), xr(d), 1).astype(BF16)
            bulk[a].append(send(xsend.at[a, d - 1], xrecv.at[a, d - 1], at(dx=d)))

    def reduce_hop(a, hop):
        for side, sign in ((0, 1), (1, -1)):
            chain[a][side][hop - 1].wait_recv()
            to = zr(sign * (4 - hop))
            if hop == 1:
                lo, hi = slice(2 * side, 2 * side + 2), slice(2 - 2 * side, 4 - 2 * side)
                ring_s[a, side, hop, lo] = (
                    part(a, to, lo, 0) + ring_r[a, side, 0, 0:2].astype(F32)
                ).astype(BF16)
                ring_s[a, side, hop, hi] = part(a, to, hi, 0).astype(BF16)
            else:
                ring_s[a, side, hop] = (
                    part(a, to, slice(0, 4), 0) + ring_r[a, side, hop - 1].astype(F32)
                ).astype(BF16)
            chain[a][side].append(
                send(ring_s.at[a, side, hop], ring_r.at[a, side, hop], at(dz=sign))
            )

    def reduce_small(a):
        for copy in bulk[a]:
            copy.wait_recv()
        total = part(a, slice(0, NZ), x, 1)
        for d in range(3):
            total = total + xrecv[a, d].astype(F32)
        r1[a] = total
        small[a] = []
        for d in (4, 3, 5, 2, 6, 1, 7):
            zsend[a, d - 1] = r1[a, zr(d)].astype(BF16)
            small[a].append(send(zsend.at[a, d - 1], zrecv.at[a, d - 1], at(dz=d)))

    def reduce_last(a):
        for side in range(2):
            chain[a][side][3].wait_recv()
        r0[a] = part(a, z, slice(0, 4), 0) + ring_r[a, 0, 3].astype(F32) + ring_r[a, 1, 3].astype(F32)
        last[a] = []
        for d in (2, 1, 3):
            x2send[a, d - 1] = r0[a, xr(d)].astype(BF16)
            last[a].append(send(x2send.at[a, d - 1], x2recv.at[a, d - 1], at(dx=d)))

    def reduce_final(a):
        for copy in small[a]:
            copy.wait_recv()
        total1 = r1[a, z]
        for d in range(7):
            total1 = total1 + zrecv[a, d].astype(F32)
        fin[a, :, :, QW:] = total1.reshape(2, 8, QW)
        for copy in last[a]:
            copy.wait_recv()
        total0 = r0[a, x]
        for d in range(3):
            total0 = total0 + x2recv[a, d].astype(F32)
        fin[a, :, :, :QW] = total0.reshape(2, 8, QW)
        final[a] = send(fin.at[a, o], finr.at[a], partner)

    for copy in far[0]:
        copy.wait_recv()
    turn(0)
    swap[0] = product(0, ((0, 2),))
    far.append(relay(2, near[2]))
    reduce_start(0)
    weight_grad(0, 1, 2, gd_hbm, 0)
    weight_grad(0, 1, 2, gd_hbm, 1)
    reduce_hop(0, 1)
    for i in range(2):
        for copy in far[1 + i]:
            copy.wait_recv()
        turn(1 + i)
    swap[1] = product(1, ((1, 0), (2, 1)))
    reduce_start(1)
    reduce_hop(0, 2)
    reduce_small(0)
    reduce_hop(1, 1)
    weight_grad(1, 0, 0, gg_hbm, 0)
    reduce_hop(0, 3)
    reduce_hop(1, 2)
    weight_grad(1, 0, 0, gg_hbm, 1)
    reduce_last(0)
    reduce_small(1)
    reduce_hop(1, 3)
    weight_grad(2, 0, 1, gu_hbm, 0)
    reduce_final(0)
    reduce_last(1)
    weight_grad(2, 0, 1, gu_hbm, 1)
    reduce_final(1)
    for a, ref in enumerate((out_ref, gtok_ref)):
        final[a].wait_recv()
        ref[:, pl.ds(pl.multiple_of(c * HW, HW), HW)] = fin[a, c].astype(BF16)
        ref[:, pl.ds(pl.multiple_of(o * HW, HW), HW)] = finr[a].astype(BF16)

    for copy in sent:
        copy.wait_send()
    for store in stores:
        store.wait()


def deliver(*refs):
    srcs, dsts, bufs, (in_sem, out_sem) = refs[:5], refs[5:10], refs[10:15], refs[15:]
    steps = []
    for i in range(5):
        load = pltpu.make_async_copy(srcs[i], bufs[i], in_sem.at[i])
        load.start()
        steps.append((load, pltpu.make_async_copy(bufs[i], dsts[i], out_sem.at[i])))
    for load, store in steps:
        load.wait()
        store.start()
    for _, store in steps:
        store.wait()


def body(tokens, gate_weight, up_weight, down_weight, gate_mask, up_mask, down_mask, grad_out):
    vmem = pl.BlockSpec(memory_space=pltpu.VMEM)
    hbm = pl.BlockSpec(memory_space=pl.ANY)
    out, gtok, gg, gu, gd = pl.pallas_call(
        kernel,
        name="ffn",
        out_shape=(
            jax.ShapeDtypeStruct((8, DL), BF16),
            jax.ShapeDtypeStruct((8, DL), BF16),
            jax.ShapeDtypeStruct((FL, DL), BF16),
            jax.ShapeDtypeStruct((FL, DL), BF16),
            jax.ShapeDtypeStruct((FL, DL), BF16),
        ),
        in_specs=[hbm] * 8,
        out_specs=(vmem, vmem, hbm, hbm, hbm),
        scratch_shapes=[
            pltpu.VMEM((2, 8, DL), BF16),
            pltpu.VMEM((3, FL // BLOCK, DL // BLOCK), jnp.int32),
            pltpu.VMEM((3, FL, DL), BF16),
            pltpu.VMEM((3, 8, DL), F32),
            pltpu.VMEM((2, 4, NZ, NX, 16, QW), BF16),
            pltpu.VMEM((2, 8, HW), F32),
            pltpu.VMEM((2, 8, HW), F32),
            pltpu.VMEM((3, FL, TOK), F32),
            pltpu.VMEM((3, FL, TOK), BF16),
            pltpu.VMEM((3, 3, SLAB, TOK), BF16),
            pltpu.VMEM((2, SLAB, TOK), F32),
            pltpu.VMEM((3, FL, TOK), BF16),
            pltpu.VMEM((3, TOK, FL), BF16),
            pltpu.VMEM((2, NZ, NX, 16, HW), F32),
            pltpu.VMEM((2, NZ, NX, 16, HW), F32),
            pltpu.VMEM((2, NZ, NX, 16, HW), F32),
            pltpu.VMEM((2, 3, NZ, 16, QW), BF16),
            pltpu.VMEM((2, 3, NZ, 16, QW), BF16),
            pltpu.VMEM((2, 3, 16, QW), BF16),
            pltpu.VMEM((2, 3, 16, QW), BF16),
            pltpu.VMEM((2, 2, 4, NX, 16, QW), BF16),
            pltpu.VMEM((2, 2, 4, NX, 16, QW), BF16),
            pltpu.VMEM((2, NX, 16, QW), F32),
            pltpu.VMEM((2, NZ, 16, QW), F32),
            pltpu.VMEM((2, 7, 16, QW), BF16),
            pltpu.VMEM((2, 7, 16, QW), BF16),
            pltpu.VMEM((2, 2, 8, HW), F32),
            pltpu.VMEM((2, 8, HW), F32),
            pltpu.VMEM((3, FL, DL), BF16),
            pltpu.SemaphoreType.DMA((N_SEMS,)),
            pltpu.SemaphoreType.DMA((N_SEMS,)),
            pltpu.SemaphoreType.DMA((11,)),
        ],
        compiler_params=pltpu.CompilerParams(
            collective_id=0, has_side_effects=True, vmem_limit_bytes=VMEM
        ),
    )(
        tokens, grad_out, gate_weight.T, up_weight.T, down_weight,
        gate_mask.T, up_mask.T, down_mask,
    )
    results = (out, gtok, gg, gu, gd)
    out, gtok, gg, gu, gd = pl.pallas_call(
        deliver,
        name="deliver",
        out_shape=tuple(jax.ShapeDtypeStruct(r.shape, r.dtype) for r in results),
        in_specs=[hbm] * 5,
        out_specs=(hbm,) * 5,
        scratch_shapes=[pltpu.VMEM(r.shape, r.dtype) for r in results]
        + [pltpu.SemaphoreType.DMA((5,)), pltpu.SemaphoreType.DMA((5,))],
        compiler_params=pltpu.CompilerParams(vmem_limit_bytes=VMEM),
    )(*results)
    return out, gtok, gg.T, gu.T, gd


def solution(mesh):
    placed = (
        P("tp", "fsdp"),
        P("fsdp", "tp"),
        P("fsdp", "tp"),
        P("tp", "fsdp"),
        P("fsdp", "tp"),
        P("fsdp", "tp"),
        P("tp", "fsdp"),
        P("tp", "fsdp"),
    )
    return jax.shard_map(
        body,
        mesh=mesh,
        in_specs=placed,
        out_specs=(
            P("tp", "fsdp"),
            P("tp", "fsdp"),
            P("fsdp", "tp"),
            P("fsdp", "tp"),
            P("tp", "fsdp"),
        ),
        check_vma=False,
    )
```

time: 110 us -> 101 us (0.918)
  local copies, waits for them, and re-layouts: 9.21 us -> 0 us
    unnamed x9 -> x0, local copies, waits for them, and re-layouts: 9.21 us -> none
    pallas_call x0 -> x1, Pallas kernels: none -> 4.34 us  [body(): pl.pallas_call(deliver, name='deliver', out_shape=tuple((jax.ShapeDtypeSt...]
    pallas_call x1, Pallas kernels: 100 us -> 96.2 us  [body(): pl.pallas_call(kernel, name='ffn', out_shape=(jax.ShapeDtypeStruct((8, DL...]
where the time goes in v2:
time: 101 us
  Pallas kernels  101 us (100%)
    pallas_call x1, Pallas kernels, body(): pl.pallas_call(kernel, name='ffn', out_shape=(jax.ShapeDtypeStruct((8, DL...  96.2 us
    pallas_call x1, Pallas kernels, body(): pl.pallas_call(deliver, name='deliver', out_shape=tuple((jax.ShapeDtypeSt...  4.34 us

profile of v2, /device:TPU:1, one launch (start us, length us, event | category | flops | bytes accessed | tf_op | source)
XLA Modules:
  0.0 101.2 jit_solution(15857397557969988086)
XLA Ops:
  0.6 96.2 %ffn.1 = (bf16[8,2048]{1,0:T(8,128)(2,1)}, bf16[8,2048]{1,0:T(8,128)(2,1)}, bf16[448,2048]{1,0:T(8,128)(2,1)}, bf16[448,2048]{1,0:T(8,128)(2,1)}, bf16[448,2048]{1,0:T(8,128)(2,1)}) custom-call(bf16[8,2048]{1,0:T(8,128)(2,1)} %tok_hbm.1, bf16[8,2048]{1,0:T(8,128)(2,1)} %cot_hbm.1, bf16[448,2048]{1,0:T(8,128)(2,1)} %bitcast.6, bf16[448,2048]{1,0:T(8,128)(2,1)} %bitcast.7, ...), custom_call_target="tpu_custom_call" | custom-call | tf_op jit(solution)/shard_map/ffn/pallas_call | solution.py:472
  96.9 4.3 %deliver.1 = (bf16[8,2048]{1,0:T(8,128)(2,1)}, bf16[8,2048]{1,0:T(8,128)(2,1)}, bf16[448,2048]{1,0:T(8,128)(2,1)}, bf16[448,2048]{1,0:T(8,128)(2,1)}, bf16[448,2048]{1,0:T(8,128)(2,1)}) custom-call(bf16[8,2048]{1,0:T(8,128)(2,1)} %get-tuple-element.15.refs_0_, bf16[8,2048]{1,0:T(8,128)(2,1)} %get-tuple-element.16.refs_1_, ...), custom_call_target="tpu_custom_call" | custom-call | tf_op jit(solution)/shard_map/deliver/pallas_call | solution.py:526

commit v3 on v2

--- a/solution.py
+++ b/solution.py
@@ -216,13 +216,13 @@
     ring_hop(0, 3)
     over_z(1)
     over_x_done(0)
-    ring_hop(1, 1)
     passed_on(0, 1)
     project(0, 0, (1, 3), False)
     ring_done(0)
     passed_on(0, 0)
     project(0, 0, (0, 2), True)
     sums = [scatter(0)]
+    ring_hop(1, 1)
     over_x(1)
     ring_hop(1, 2)
     project(1, 0, (0, 1, 2, 3), True)
@@ -420,19 +420,21 @@
     weight_grad(0, 1, 2, gd_hbm, 0)
     weight_grad(0, 1, 2, gd_hbm, 1)
     reduce_hop(0, 1)
-    for i in range(2):
-        for copy in far[1 + i]:
-            copy.wait_recv()
-        turn(1 + i)
+    for copy in far[1]:
+        copy.wait_recv()
+    turn(1)
+    weight_grad(1, 0, 0, gg_hbm, 0)
+    weight_grad(1, 0, 0, gg_hbm, 1)
+    for copy in far[2]:
+        copy.wait_recv()
+    turn(2)
     swap[1] = product(1, ((1, 0), (2, 1)))
     reduce_start(1)
     reduce_hop(0, 2)
     reduce_small(0)
     reduce_hop(1, 1)
-    weight_grad(1, 0, 0, gg_hbm, 0)
     reduce_hop(0, 3)
     reduce_hop(1, 2)
-    weight_grad(1, 0, 0, gg_hbm, 1)
     reduce_last(0)
     reduce_small(1)
     reduce_hop(1, 3)

time: 101 us -> 104 us (1.030)
  Pallas kernels: 101 us -> 103 us
    pallas_call x1, Pallas kernels: 96.2 us -> 98.6 us  [body(): pl.pallas_call(kernel, name='ffn', out_shape=(jax.ShapeDtypeStruct((8, DL...]
where the time goes in v3:
time: 104 us
  Pallas kernels  103 us (99%)
    pallas_call x1, Pallas kernels, body(): pl.pallas_call(kernel, name='ffn', out_shape=(jax.ShapeDtypeStruct((8, DL...  98.6 us
    pallas_call x1, Pallas kernels, body(): pl.pallas_call(deliver, name='deliver', out_shape=tuple((jax.ShapeDtypeSt...  4.34 us

profile of v3, /device:TPU:1, one launch (start us, length us, event | category | flops | bytes accessed | tf_op | source)
XLA Modules:
  0.0 103.6 jit_solution(13967970506051706059)
XLA Ops:
  0.6 98.6 %ffn.1 = (bf16[8,2048]{1,0:T(8,128)(2,1)}, bf16[8,2048]{1,0:T(8,128)(2,1)}, bf16[448,2048]{1,0:T(8,128)(2,1)}, bf16[448,2048]{1,0:T(8,128)(2,1)}, bf16[448,2048]{1,0:T(8,128)(2,1)}) custom-call(bf16[8,2048]{1,0:T(8,128)(2,1)} %tok_hbm.1, bf16[8,2048]{1,0:T(8,128)(2,1)} %cot_hbm.1, bf16[448,2048]{1,0:T(8,128)(2,1)} %bitcast.6, bf16[448,2048]{1,0:T(8,128)(2,1)} %bitcast.7, ...), custom_call_target="tpu_custom_call" | custom-call | tf_op jit(solution)/shard_map/ffn/pallas_call | solution.py:474
  99.2 4.3 %deliver.1 = (bf16[8,2048]{1,0:T(8,128)(2,1)}, bf16[8,2048]{1,0:T(8,128)(2,1)}, bf16[448,2048]{1,0:T(8,128)(2,1)}, bf16[448,2048]{1,0:T(8,128)(2,1)}, bf16[448,2048]{1,0:T(8,128)(2,1)}) custom-call(bf16[8,2048]{1,0:T(8,128)(2,1)} %get-tuple-element.15.refs_0_, bf16[8,2048]{1,0:T(8,128)(2,1)} %get-tuple-element.16.refs_1_, ...), custom_call_target="tpu_custom_call" | custom-call | tf_op jit(solution)/shard_map/deliver/pallas_call | solution.py:528
